TPU v7x, 32 devices: a whole 2x2x4 slice. The times are simulated.
32 devices in a mesh: dp: 4 (over y, x), expert: 8 (over z, core).
Axes of the slice: x: 2, y: 2, z: 4, core: 2. Of those that a mesh axis runs over, the one named last changes fastest.
Arguments:
- tokens: bfloat16 [4096, 2048], P(('dp', 'expert')), may hold values from -6 to 6
- out_grad: bfloat16 [4096, 2048], P(('dp', 'expert')), may hold values from -6 to 6
- expert_ids: int32 [4096, 8], P(('dp', 'expert')), may hold values from 0 to 15, all different within a row; in each aligned block of 128 rows (0 to 127, 128 to 255, ...) at most 72 rows name the same one
- route_probs: float32 [4096, 8], P(('dp', 'expert')), may hold values from 0.05 to 0.5
- gate_weight: bfloat16 [16, 2048, 384], P('expert'), may hold values from -0.125 to 0.125
- up_weight: bfloat16 [16, 2048, 384], P('expert'), may hold values from -0.125 to 0.125
- down_weight: bfloat16 [16, 384, 2048], P('expert'), may hold values from -0.3125 to 0.3125
Outputs:
- in_grad: bfloat16 [4096, 2048], P(('dp', 'expert'))
- grad_gate: bfloat16 [16, 2048, 384], P('expert', 'dp')
- grad_up: bfloat16 [16, 2048, 384], P('expert', 'dp')
- grad_down: bfloat16 [16, 384, 2048], P('expert', None, 'dp')
Inputs may be any that keep to these rules, and one draw needn't show every extreme that they name: `expert_ids`: within the 128 tokens of one device no expert is named more than 72 times, a bound that some block reaches; a token names 8 different experts.
All inputs are finite; a program needn't handle non-finite values.
Results may differ from a plain program's by a relative error of at most 0.014.
Values may be sent and summed in bfloat16 or wider, within the bound.
A program may use at most 128 MiB of HBM per device.

v0:
```python
import jax
import jax.numpy as jnp
from jax import lax
from jax.sharding import PartitionSpec as P


def contract(left, right, left_dim, right_dim):
    return lax.dot_general(
        left, right, (((left_dim,), (right_dim,)), ((), ())), preferred_element_type=jnp.float32
    )


def expert_work(xr, scaled, w_gate, w_up, w_down):
    gate = jnp.dot(xr, w_gate, preferred_element_type=jnp.float32)
    up = jnp.dot(xr, w_up, preferred_element_type=jnp.float32)
    sig = jax.nn.sigmoid(gate)
    act = (gate * sig * up).astype(jnp.bfloat16)
    dh = contract(scaled, w_down, 1, 1)
    dgate = (dh * up * sig * (1.0 + gate * (1.0 - sig))).astype(jnp.bfloat16)
    dup = (dh * gate * sig).astype(jnp.bfloat16)
    contrib = (contract(dgate, w_gate, 1, 1) + contract(dup, w_up, 1, 1)).astype(jnp.bfloat16)
    grad_g = contract(xr, dgate, 0, 0).astype(jnp.bfloat16)
    grad_u = contract(xr, dup, 0, 0).astype(jnp.bfloat16)
    grad_d = contract(act, scaled, 0, 0).astype(jnp.bfloat16)
    return (contrib, grad_g, grad_u, grad_d)


def per_device(tokens, out_grad, expert_ids, route_probs, gate_weight, up_weight, down_weight):
    tok_dev, width = tokens.shape
    top_k = expert_ids.shape[1]
    exp_dev = gate_weight.shape[0]
    n_owner = lax.axis_size("expert")
    experts = exp_dev * n_owner
    slots = tok_dev * top_k * 9 // (experts * 8)
    pairs = tok_dev * top_k
    flat = expert_ids.reshape(-1)
    columns = jnp.arange(experts, dtype=jnp.int32)
    onehot = (flat[:, None] == columns[None, :]).astype(jnp.int32)
    rank = jnp.sum(jnp.cumsum(onehot, axis=0) * onehot, axis=1) - 1
    dest = flat * slots + rank
    table = jnp.full((experts * slots,), pairs, dtype=jnp.int32)
    table = table.at[dest].set(jnp.arange(pairs, dtype=jnp.int32))
    tok_index = table // top_k
    zero_row = jnp.zeros((1, width), dtype=jnp.bfloat16)
    x_pad = jnp.concatenate([tokens, zero_row], axis=0)
    dy_pad = jnp.concatenate([out_grad, zero_row], axis=0)
    p_pad = jnp.concatenate([route_probs.reshape(-1), jnp.zeros((1,), dtype=jnp.float32)], axis=0)
    send_x = x_pad[tok_index]
    send_dy = (p_pad[table][:, None] * dy_pad[tok_index].astype(jnp.float32)).astype(jnp.bfloat16)
    send_x = send_x.reshape(n_owner, exp_dev * slots, width)
    send_dy = send_dy.reshape(n_owner, exp_dev * slots, width)
    recv_x, recv_dy = (
        lax.all_to_all(send_x, "expert", split_axis=0, concat_axis=0, tiled=True),
        lax.all_to_all(send_dy, "expert", split_axis=0, concat_axis=0, tiled=True),
    )
    recv_x = recv_x.reshape(n_owner, exp_dev, slots, width)
    recv_dy = recv_dy.reshape(n_owner, exp_dev, slots, width)
    contribs = []
    gates = []
    ups = []
    downs = []
    for local in range(exp_dev):
        xr = recv_x[:, local].reshape(n_owner * slots, width)
        scaled = recv_dy[:, local].reshape(n_owner * slots, width)
        contrib, grad_g, grad_u, grad_d = expert_work(
            xr, scaled, gate_weight[local], up_weight[local], down_weight[local]
        )
        contribs.append(contrib.reshape(n_owner, slots, width))
        gates.append(grad_g)
        ups.append(grad_u)
        downs.append(grad_d)
    back = jnp.stack(contribs, axis=1).reshape(n_owner, exp_dev * slots, width)
    returned = lax.all_to_all(back, "expert", split_axis=0, concat_axis=0, tiled=True)
    returned = returned.reshape(experts * slots, width)
    rows = returned[dest].reshape(tok_dev, top_k, width)
    in_grad = jnp.sum(rows.astype(jnp.float32), axis=1).astype(jnp.bfloat16)
    stack_g = jnp.stack(gates, axis=0)
    stack_u = jnp.stack(ups, axis=0)
    stack_d = jnp.stack(downs, axis=0)
    stack_g, stack_u, stack_d = (
        lax.psum_scatter(stack_g, "dp", scatter_dimension=1, tiled=True).astype(jnp.float32),
        lax.psum_scatter(stack_u, "dp", scatter_dimension=1, tiled=True).astype(jnp.float32),
        lax.psum_scatter(stack_d, "dp", scatter_dimension=2, tiled=True).astype(jnp.float32),
    )
    stack_g = stack_g.astype(jnp.bfloat16)
    stack_u = stack_u.astype(jnp.bfloat16)
    stack_d = stack_d.astype(jnp.bfloat16)
    return (in_grad, stack_g, stack_u, stack_d)


def solution(mesh):
    in_specs = (
        P(("dp", "expert"), None),
        P(("dp", "expert"), None),
        P(("dp", "expert"), None),
        P(("dp", "expert"), None),
        P("expert", None, None),
        P("expert", None, None),
        P("expert", None, None),
    )
    out_specs = (
        P(("dp", "expert"), None),
        P("expert", "dp", None),
        P("expert", "dp", None),
        P("expert", None, "dp"),
    )
    return jax.shard_map(
        per_device, mesh=mesh, in_specs=in_specs, out_specs=out_specs, check_vma=False
    )
```

profile of v0, /device:TPU:0, one launch (start us, length us, event | category | flops | bytes accessed | tf_op | source)
XLA Modules:
  0.0 416.0 jit_solution(10283504415113785305)
XLA Ops:
  7.2 0.7 broadcast_multiply_fusion
  7.9 0.8 copy.15
  8.6 0.1 eq.29
  8.7 0.1 eq.25
  8.8 0.1 copy.14
  8.9 0.1 mul.80
  9.0 4.5 %reduce-window.6 = s32[16,8,128]{2,1,0:T(8,128)S(1)} reduce-window(s32[16,8,128]{2,1,0:T(8,128)S(1)} %fusion.39, s32[]{:T(128)} %constant.17.clone.1), window={size=1x1x128 pad=0_0x0_0x127_0}, to_apply=%region_0.0 | reduce-window | flops 2080768 | bytes 131076 | tf_op jit(solution)/shard_map/reduce-window
  13.6 0.1 slice.56
  13.6 0.1 copy.17
  13.8 0.1 copy.18
  13.9 0.1 broadcast_add_fusion
  14.0 4.3 %scatter_custom_fusion = s32[1152]{0:T(1024)S(1)} fusion(s32[1024]{0:T(1024)S(1)} %bitcast.117, s32[1024]{0:T(1024)S(1)} %iota.11, s32[]{:T(128)} %constant.14.clone.1), kind=kCustom, calls=%fused_computation.84 | custom fusion | bytes 4612 | tf_op jit(solution)/shard_map/scatter | solution.py:42
  18.4 1.1 concatenate.11
  19.5 6.0 %gather_fusion.2 = bf16[1152,2048]{1,0:T(8,128)(2,1)} fusion(bf16[129,2048]{1,0:T(8,128)(2,1)S(1)} %concatenate.11, s32[2048]{0:T(1024)S(1)} %get-tuple-element.14), kind=kCustom, calls=%fused_computation.2 | custom fusion | bytes 9441792 | tf_op jit(solution)/shard_map/gather | solution.py:48
  25.5 6.5 %all-to-all-start.1 = ((bf16[8,144,2048]{2,1,0:T(8,128)(2,1)}), bf16[8,144,2048]{2,1,0:T(8,128)(2,1)}, u32[]{:S(2)}, u32[]{:S(2)}) async-start(bf16[8,144,2048]{2,1,0:T(8,128)(2,1)} %bitcast.99), calls=%async_computation.1 | async-start | bytes 9437184 | tf_op jit(solution)/shard_map/all_to_all | solution.py:53
  31.9 0.1 copy.13
  32.0 0.1 reshape.90
  32.1 6.5 %gather_fusion = f32[1152]{0:T(1024)S(1)} fusion(f32[1025]{0:T(1024)S(1)} %pad_maximum_fusion.4, s32[2048]{0:T(1024)S(1)} %get-tuple-element.15), kind=kCustom, calls=%fused_computation | custom fusion | bytes 13824 | tf_op jit(solution)/shard_map/gather | solution.py:49
  38.6 0.1 mul.82
  38.8 5.9 %gather_fusion.1 = bf16[1152,2048]{1,0:T(8,128)(2,1)} fusion(bf16[129,2048]{1,0:T(8,128)(2,1)S(1)} %concatenate.10, s32[2048]{0:T(1024)S(1)} %get-tuple-element.14), kind=kCustom, calls=%fused_computation.1 | custom fusion | bytes 9441792 | tf_op jit(solution)/shard_map/gather | solution.py:49
  44.7 5.4 %fusion = bf16[8,144,2048]{2,1,0:T(8,128)(2,1)} fusion(bf16[8,144,2048]{2,1,0:T(8,128)(2,1)} %bitcast.100, f32[8,144]{1,0:T(8,128)S(1)} %mul.82), kind=kLoop, calls=%fused_computation.6 | loop fusion | flops 7077888 | bytes 9441792 | tf_op jit(solution)/shard_map/convert_element_type | solution.py:49
  50.0 87.2 %all-to-all-done.1 = bf16[8,144,2048]{2,1,0:T(8,128)(2,1)} async-done(((bf16[8,144,2048]{2,1,0:T(8,128)(2,1)}), bf16[8,144,2048]{2,1,0:T(8,128)(2,1)}, u32[]{:S(2)}, u32[]{:S(2)}) %all-to-all-start.1) | async-done | bytes 4718624 | tf_op jit(solution)/shard_map/all_to_all | solution.py:53
  137.3 4.6 %all-to-all-start = ((bf16[8,144,2048]{2,1,0:T(8,128)(2,1)}), bf16[8,144,2048]{2,1,0:T(8,128)(2,1)}, u32[]{:S(2)}, u32[]{:S(2)}) async-start(bf16[8,144,2048]{2,1,0:T(8,128)(2,1)} %fusion), calls=%async_computation | async-start | bytes 9437184 | tf_op jit(solution)/shard_map/all_to_all | solution.py:54
  141.9 0.2 reduce-scatter.8.cloned.1.call-start
  142.1 2.9 fusion.47
  145.0 0.4 copy-done
  145.4 2.3 fusion.9
  147.7 1.2 copy-done.1
  148.9 2.3 fusion.12
  151.2 2.3 fusion.18
  153.6 2.3 fusion.21
  155.9 91.2 %all-to-all-done = bf16[8,144,2048]{2,1,0:T(8,128)(2,1)} async-done(((bf16[8,144,2048]{2,1,0:T(8,128)(2,1)}), bf16[8,144,2048]{2,1,0:T(8,128)(2,1)}, u32[]{:S(2)}, u32[]{:S(2)}) %all-to-all-start) | async-done | bytes 4718624 | tf_op jit(solution)/shard_map/all_to_all | solution.py:54
  247.1 2.9 fusion.46
  250.1 1.5 fusion.5
  251.6 0.7 copy-done.10
  252.2 0.6 copy-done.26
  252.8 1.5 fusion.6
  254.3 1.9 pad_maximum_fusion.3
  256.3 0.3 reduce-scatter.6.cloned.1.call-start
  256.5 5.1 %multiply_convert_fusion.2 = (bf16[576,384]{1,0:T(8,128)(2,1)S(1)}, bf16[576,384]{1,0:T(8,128)(2,1)}) fusion(f32[576,384]{1,0:T(8,128)} %fusion.9, f32[576,384]{1,0:T(8,128)} %fusion.12, bf16[576,2048]{1,0:T(8,128)(2,1)} %bitcast.114, bf16[2,384,2048]{2,1,0:T(8,128)(2,1)} %param.13), kind=kOutput, calls=%fused_computation.56 | convolution fusion | flops 908845056 | bytes 6586368 | tf_op jit(solution)/shard_map/dot_general | solution.py:8
  261.7 1.7 fusion.4
  263.4 0.1 copy-done.9
  263.5 0.9 copy-done.20
  264.4 0.2 copy-done.22
  264.6 0.3 copy-done.24
  264.9 2.4 multiply_convert_fusion.4
  267.3 0.8 copy-done.17
  268.0 1.7 fusion.3
  269.8 2.1 pad_maximum_fusion.2
  271.9 2.5 fusion.16
  274.4 1.4 fusion.7
  275.9 0.5 copy-done.2
  276.3 0.1 copy-done.18
  276.4 1.4 add_convert_fusion.1
  277.9 1.4 add_convert_fusion
  279.3 2.5 pad_maximum_fusion
  281.8 4.7 %all-to-all-start.2 = ((bf16[8,144,2048]{2,1,0:T(8,128)(2,1)}), bf16[8,144,2048]{2,1,0:T(8,128)(2,1)}, u32[]{:S(2)}, u32[]{:S(2)}) async-start(bf16[8,144,2048]{2,1,0:T(8,128)(2,1)} %bitcast.98), calls=%async_computation.2 | async-start | bytes 9437184 | tf_op jit(solution)/shard_map/all_to_all | solution.py:73
  286.6 0.3 reduce-scatter.4.cloned.1.call-start
  286.9 4.0 fusion.2
  291.0 1.7 fusion.1
  292.7 2.0 pad_maximum_fusion.1
  294.7 97.1 %all-to-all-done.2 = bf16[8,144,2048]{2,1,0:T(8,128)(2,1)} async-done(((bf16[8,144,2048]{2,1,0:T(8,128)(2,1)}), bf16[8,144,2048]{2,1,0:T(8,128)(2,1)}, u32[]{:S(2)}, u32[]{:S(2)}) %all-to-all-start.2) | async-done | bytes 4718624 | tf_op jit(solution)/shard_map/all_to_all | solution.py:73
  391.8 11.8 %gather_fusion.3 = bf16[1024,2048]{1,0:T(8,128)(2,1)} fusion(bf16[1152,2048]{1,0:T(8,128)(2,1)} %bitcast.23, s32[1024]{0:T(1024)S(1)} %broadcast_clamp_fusion), kind=kCustom, calls=%fused_computation.3 | custom fusion | bytes 8392704 | tf_op jit(solution)/shard_map/gather | solution.py:75
  403.6 5.9 %bitcast_reduce_fusion = bf16[128,2048]{1,0:T(8,128)(2,1)} fusion(bf16[1024,2048]{1,0:T(8,128)(2,1)} %gather_fusion.3), kind=kLoop, calls=%fused_computation.10 | loop fusion | flops 1835008 | bytes 4718592 | tf_op jit(solution)/shard_map/reduce_sum | solution.py:76
  (61 shorter events, 0.3 us)
Async XLA Ops:
  25.5 6.5 %copy-start.19 = (f32[128,8]{0,1:T(8,128)S(1)}, f32[128,8]{0,1:T(8,128)}, u32[]{:S(2)}) copy-start(f32[128,8]{0,1:T(8,128)} %param.10) | copy-start | bytes 12292
  25.5 111.8 %all-to-all-start.1 = ((bf16[8,144,2048]{2,1,0:T(8,128)(2,1)}), bf16[8,144,2048]{2,1,0:T(8,128)(2,1)}, u32[]{:S(2)}, u32[]{:S(2)}) async-start(bf16[8,144,2048]{2,1,0:T(8,128)(2,1)} %bitcast.99), calls=%async_computation.1 | async-start | bytes 9437184 | tf_op jit(solution)/shard_map/all_to_all | solution.py:53
  32.1 6.6 %copy-start.14 = (bf16[128,2048]{1,0:T(8,128)(2,1)S(1)}, bf16[128,2048]{1,0:T(8,128)(2,1)}, u32[]{:S(2)}) copy-start(bf16[128,2048]{1,0:T(8,128)(2,1)} %param.8) | copy-start | bytes 1572868
  137.3 109.8 %all-to-all-start = ((bf16[8,144,2048]{2,1,0:T(8,128)(2,1)}), bf16[8,144,2048]{2,1,0:T(8,128)(2,1)}, u32[]{:S(2)}, u32[]{:S(2)}) async-start(bf16[8,144,2048]{2,1,0:T(8,128)(2,1)} %fusion), calls=%async_computation | async-start | bytes 9437184 | tf_op jit(solution)/shard_map/all_to_all | solution.py:54
  141.9 267.6 %reduce-scatter.8.cloned.1.call-start = ((), (), s32[]{:S(2)}) async-start(), calls=%async_computation.8 | async-start | bytes 3932160 | tf_op jit(solution)/shard_map/reduce_scatter | solution.py:83
  142.1 3.3 copy-start
  145.0 2.7 copy-start.6
  145.0 8.5 %copy-start.3 = (bf16[8,1,72,2048]{3,2,1,0:T(8,128)(2,1)}, bf16[8,1,72,2048]{3,2,1,0:T(8,128)(2,1)S(1)}, u32[]{:S(2)}) copy-start(bf16[8,1,72,2048]{3,2,1,0:T(8,128)(2,1)S(1)} %get-tuple-element.6) | copy-start | bytes 7077892
  145.4 3.5 copy-start.1
  247.1 2.9 copy-start.21
  247.1 2.9 copy-start.23
  250.0 1.6 copy-start.8
  250.0 2.2 copy-start.10
  250.0 2.2 copy-start.25
  250.0 2.8 copy-start.26
  256.3 153.3 %reduce-scatter.6.cloned.1.call-start = ((), (), s32[]{:S(2)}) async-start(), calls=%async_computation.7 | async-start | bytes 3932160 | tf_op jit(solution)/shard_map/reduce_scatter | solution.py:82
  256.5 5.1 %copy-start.7 = (bf16[8,1,72,2048]{3,2,1,0:T(8,128)(2,1)S(1)}, bf16[8,1,72,2048]{3,2,1,0:T(8,128)(2,1)}, u32[]{:S(2)}) copy-start(bf16[8,1,72,2048]{3,2,1,0:T(8,128)(2,1)} %copy-done.6) | copy-start | bytes 7077892
  261.6 1.8 copy-start.15
  261.6 1.9 copy-start.9
  261.6 2.8 copy-start.20
  261.7 3.0 copy-start.22
  261.7 3.2 copy-start.24
  264.9 3.1 copy-start.4
  267.3 0.8 copy-start.17
  271.9 2.5 copy-start.11
  274.4 1.9 copy-start.2
  274.4 2.0 copy-start.18
  276.4 1.4 copy-start.16
  281.8 5.1 %copy-start.12 = (bf16[576,384]{1,0:T(8,128)(2,1)S(1)}, bf16[576,384]{1,0:T(8,128)(2,1)}, u32[]{:S(2)}) copy-start(bf16[576,384]{1,0:T(8,128)(2,1)} %get-tuple-element.11) | copy-start | bytes 1327108
  281.8 110.0 %all-to-all-start.2 = ((bf16[8,144,2048]{2,1,0:T(8,128)(2,1)}), bf16[8,144,2048]{2,1,0:T(8,128)(2,1)}, u32[]{:S(2)}, u32[]{:S(2)}) async-start(bf16[8,144,2048]{2,1,0:T(8,128)(2,1)} %bitcast.98), calls=%async_computation.2 | async-start | bytes 9437184 | tf_op jit(solution)/shard_map/all_to_all | solution.py:73
  286.6 4.4 %copy-start.5 = (bf16[8,1,72,2048]{3,2,1,0:T(8,128)(2,1)S(1)}, bf16[8,1,72,2048]{3,2,1,0:T(8,128)(2,1)}, u32[]{:S(2)}) copy-start(bf16[8,1,72,2048]{3,2,1,0:T(8,128)(2,1)} %copy-done.3) | copy-start | bytes 7077892
  286.6 4.4 %copy-start.13 = (bf16[576,384]{1,0:T(8,128)(2,1)S(1)}, bf16[576,384]{1,0:T(8,128)(2,1)}, u32[]{:S(2)}) copy-start(bf16[576,384]{1,0:T(8,128)(2,1)} %get-tuple-element.9) | copy-start | bytes 1327108
  286.6 122.9 %reduce-scatter.4.cloned.1.call-start = ((), (), s32[]{:S(2)}) async-start(), calls=%async_computation.6 | async-start | bytes 3932160 | tf_op jit(solution)/shard_map/reduce_scatter | solution.py:81
Sparse Core Ops, SparseCore 0:
  256.4 42.8 reduce-scatter.7
  302.8 43.9 reduce-scatter.5
  350.3 43.9 reduce-scatter.3
where the time goes:
time: 417 us; the launch traced here: 416 us
  waiting for transfers between devices  276 us (66%)
  local copies, waits for them, and re-layouts  48.8 us (12%)
  matrix products  35.7 us (9%)
  other arithmetic  25.2 us (6%)
  starting transfers between devices  16.6 us (4%)
  between operations  14.2 us (3%)
    all_to_all x1, waiting for transfers between devices, per_device(): lax.all_to_all(back, 'expert', split_axis=0, concat_axis=0, tiled=True)  97.1 us
    all_to_all x1, waiting for transfers between devices, per_device(): lax.all_to_all(send_dy, 'expert', split_axis=0, concat_axis=0, tiled=True)  91.2 us
    all_to_all x1, waiting for transfers between devices, per_device(): lax.all_to_all(send_x, 'expert', split_axis=0, concat_axis=0, tiled=True)  87.2 us
    dot_general x12, matrix products, contract(): lax.dot_general(left, right, (((left_dim,), (right_dim,)), ((), ())), pre...  26.4 us
    gather x1, local copies, waits for them, and re-layouts, per_device(): rows = returned[dest].reshape(tok_dev, top_k, width)  11.8 us
  transfers between devices with their start and end apart: 6, of which 3 were waited for; matrix products, arithmetic and copies ran while one was open for 19% of the time, Pallas kernels for 0%

commit v1 on v0

v1 whole, which is shorter than its diff:
```python
import jax
import jax.numpy as jnp
from jax import lax
from jax.sharding import PartitionSpec as P


def contract(left, right, left_dim, right_dim):
    return lax.dot_general(
        left, right, (((left_dim,), (right_dim,)), ((), ())), preferred_element_type=jnp.float32
    )


def per_device(tokens, out_grad, expert_ids, route_probs, gate_weight, up_weight, down_weight):
    width = tokens.shape[1]
    exp_dev, _, hid = gate_weight.shape
    bf16 = jnp.bfloat16
    n_owner = lax.axis_size("expert")
    experts = exp_dev * n_owner
    columns = jnp.arange(experts, dtype=jnp.int32)
    hit = expert_ids[:, :, None] == columns[None, None, :]
    weight = jnp.sum(jnp.where(hit, route_probs[:, :, None], 0.0), axis=1)
    first = lax.axis_index("expert") * exp_dev
    all_weight = lax.all_gather(weight, "expert", axis=0, tiled=True)
    mine = lax.dynamic_slice_in_dim(all_weight, first, exp_dev, axis=1)
    x = lax.all_gather(tokens, "expert", axis=0, tiled=True)
    dy = lax.all_gather(out_grad, "expert", axis=0, tiled=True)
    w_gate = jnp.concatenate([gate_weight[e] for e in range(exp_dev)], axis=1)
    w_up = jnp.concatenate([up_weight[e] for e in range(exp_dev)], axis=1)
    w_down = down_weight.reshape(exp_dev * hid, width)
    prob = jnp.repeat(mine, hid, axis=1)
    gate = contract(x, w_gate, 1, 0)
    up = contract(x, w_up, 1, 0)
    sig = jax.nn.sigmoid(gate)
    silu = gate * sig
    slope = up * sig * (1.0 + gate * (1.0 - sig))
    dh = contract(dy, w_down, 1, 1) * prob
    act = (silu * up * prob).astype(bf16)
    dgate = (dh * slope).astype(bf16)
    dup = (dh * silu).astype(bf16)
    grad_d = contract(act, dy, 0, 0).astype(bf16).reshape(exp_dev, hid, width)
    grad_g = contract(x, dgate, 0, 0).astype(bf16)
    grad_u = contract(x, dup, 0, 0).astype(bf16)
    grad_g = jnp.stack([grad_g[:, e * hid:(e + 1) * hid] for e in range(exp_dev)], axis=0)
    grad_u = jnp.stack([grad_u[:, e * hid:(e + 1) * hid] for e in range(exp_dev)], axis=0)
    part = (contract(dgate, w_gate, 1, 1) + contract(dup, w_up, 1, 1)).astype(bf16)
    in_grad = lax.psum_scatter(part, "expert", scatter_dimension=0, tiled=True)
    grad_d = lax.psum_scatter(grad_d, "dp", scatter_dimension=2, tiled=True)
    grad_g = lax.psum_scatter(grad_g, "dp", scatter_dimension=1, tiled=True)
    grad_u = lax.psum_scatter(grad_u, "dp", scatter_dimension=1, tiled=True)
    return (in_grad, grad_g, grad_u, grad_d)


def solution(mesh):
    in_specs = (
        P(("dp", "expert"), None),
        P(("dp", "expert"), None),
        P(("dp", "expert"), None),
        P(("dp", "expert"), None),
        P("expert", None, None),
        P("expert", None, None),
        P("expert", None, None),
    )
    out_specs = (
        P(("dp", "expert"), None),
        P("expert", "dp", None),
        P("expert", "dp", None),
        P("expert", None, "dp"),
    )
    return jax.shard_map(
        per_device, mesh=mesh, in_specs=in_specs, out_specs=out_specs, check_vma=False
    )
```

time: 417 us -> 321 us (0.77)
  waiting for transfers between devices: 276 us -> 211 us
  local copies, waits for them, and re-layouts: 48.8 us -> 20.5 us
  other arithmetic: 25.2 us -> 4.66 us
  matrix products: 35.7 us -> 54.2 us
  starting transfers between devices: 16.6 us -> 0.24 us
  blocking collectives: 0 us -> 15.8 us
    all_to_all x3 -> x0, waiting for transfers between devices: 276 us -> none  [the longest x1 97.1 us: per_device(): lax.all_to_all(back, 'expert', split_axis=0, concat_axis=0, tiled=True)]
    reduce_scatter x3 -> x4, waiting for transfers between devices: 0.01 us -> 153 us  [the longest x1 52.7 us: per_device(): in_grad = lax.psum_scatter(part, 'expert', scatter_dimension=0, tiled=True)]
    all_gather x0 -> x2, waiting for transfers between devices: none -> 56.2 us  [the longest x1 34.1 us: per_device(): dy = lax.all_gather(out_grad, 'expert', axis=0, tiled=True)]
    gather x4 -> x0, local copies, waits for them, and re-layouts: 30.1 us -> none  [the longest x1 11.8 us: per_device(): rows = returned[dest].reshape(tok_dev, top_k, width)]
    dot_general x12 -> x8, matrix products: 26.4 us -> 54.2 us  [contract(): lax.dot_general(left, right, (((left_dim,), (right_dim,)), ((), ())), pre...]
    all_to_all x3 -> x0, starting transfers between devices: 15.8 us -> none  [the longest x1 6.46 us: per_device(): lax.all_to_all(send_x, 'expert', split_axis=0, concat_axis=0, tiled=True)]
    all_gather x0 -> x1, blocking collectives: none -> 15.8 us  [per_device(): all_weight = lax.all_gather(weight, 'expert', axis=0, tiled=True)]
    dot_general x4 -> x0, matrix products: 9.29 us -> none  [the longest x2 4.66 us: expert_work(): up = jnp.dot(xr, w_up, preferred_element_type=jnp.float32)]
  transfers between devices with their start and end apart: 6 -> 6, of which waited for: 3 -> 6; matrix products, arithmetic and copies ran while one was open for 19% -> 18% of each run, Pallas kernels for 0% -> 0%
where the time goes in v1:
time: 321 us; the launch traced here: 320 us
  waiting for transfers between devices  211 us (66%)
  matrix products  54.2 us (17%)
  local copies, waits for them, and re-layouts  20.5 us (6%)
  blocking collectives  15.8 us (5%)
  between operations  14.3 us (4%)
  other arithmetic  4.66 us (1%)
    dot_general x8, matrix products, contract(): lax.dot_general(left, right, (((left_dim,), (right_dim,)), ((), ())), pre...  54.2 us
    reduce_scatter x1, waiting for transfers between devices, per_device(): in_grad = lax.psum_scatter(part, 'expert', scatter_dimension=0, tiled=True)  52.7 us
    reduce_scatter x1, waiting for transfers between devices, per_device(): grad_d = lax.psum_scatter(grad_d, 'dp', scatter_dimension=2, tiled=True)  45.1 us
    reduce_scatter x1, waiting for transfers between devices, per_device(): grad_g = lax.psum_scatter(grad_g, 'dp', scatter_dimension=1, tiled=True)  44.5 us
    all_gather x1, waiting for transfers between devices, per_device(): dy = lax.all_gather(out_grad, 'expert', axis=0, tiled=True)  34.1 us
    all_gather x1, waiting for transfers between devices, per_device(): x = lax.all_gather(tokens, 'expert', axis=0, tiled=True)  22.1 us
    all_gather x1, blocking collectives, per_device(): all_weight = lax.all_gather(weight, 'expert', axis=0, tiled=True)  15.8 us
    unnamed x31, local copies, waits for them, and re-layouts  11.8 us
  transfers between devices with their start and end apart: 6, of which 6 were waited for; matrix products, arithmetic and copies ran while one was open for 18% of the time, Pallas kernels for 0%

profile of v1, /device:TPU:0, one launch (start us, length us, event | category | flops | bytes accessed | tf_op | source)
XLA Modules:
  0.0 320.4 jit_solution(6909183126216537228)
XLA Ops:
  7.2 0.0 copy-start
  7.2 0.0 all-gather.5.cloned.1.call-start
  7.2 0.7 all-gather.5.cloned.1.call-update
  7.9 0.0 all-gather.3.cloned.1.call-start
  8.0 0.7 all-gather.3.cloned.1.call-update
  8.7 0.0 reduce-scatter.9.cloned.1.call-start
  8.7 0.7 select_reduce_fusion
  9.4 15.8 %all_gather.10 = f32[1024,16]{0,1:T(8,128)S(1)} all-gather(f32[128,16]{0,1:T(8,128)S(1)} %select_reduce_fusion), channel_id=1, replica_groups=mesh['dp'=4,'expert'=8] {'expert'}, dimensions={0}, use_global_device_ids=true | all-gather | bytes 73728 | tf_op jit(solution)/shard_map/all_gather | solution.py:23
  25.2 1.0 copy.17
  26.2 3.1 broadcast_in_dim.20
  29.3 0.0 copy-start.2
  29.4 1.9 copy.24
  31.3 1.1 copy-done.2
  32.4 0.0 copy-start.3
  32.4 2.1 slice_bitcast_fusion.5
  34.4 1.0 copy-done.3
  35.4 2.0 slice_bitcast_fusion.7
  37.5 22.1 %all-gather.5.cloned.1.call-done = bf16[1024,2048]{1,0:T(8,128)(2,1)} async-done(((bf16[128,2048]{1,0:T(8,128)(2,1)}), bf16[1024,2048]{1,0:T(8,128)(2,1)}) %all-gather.5.cloned.1.call-update) | async-done | bytes 4194320 | tf_op jit(solution)/shard_map/all_gather | solution.py:25
  59.6 0.0 copy-start.5
  59.6 0.0 copy-start.7
  59.6 0.0 copy-start.9
  59.6 8.3 %fusion.12 = f32[768,1024]{0,1:T(8,128)} fusion(bf16[1024,2048]{1,0:T(8,128)(2,1)} %all-gather.5.cloned.1.call-done, bf16[2048,384]{1,0:T(8,128)(2,1)} %get-tuple-element.21, bf16[2048,384]{1,0:T(8,128)(2,1)} %get-tuple-element.20), kind=kOutput, calls=%fused_computation.26 | convolution fusion | flops 3227516928 | bytes 10485760 | tf_op jit(solution)/shard_map/dot_general | solution.py:8
  67.9 0.0 copy-done.5
  67.9 0.0 copy-done.7
  67.9 0.0 copy-done.9
  67.9 5.0 %fusion.13 = f32[768,1024]{0,1:T(8,128)} fusion(bf16[1024,2048]{1,0:T(8,128)(2,1)S(1)} %copy-done.9, bf16[2048,384]{1,0:T(8,128)(2,1)S(1)} %copy-done.7, bf16[2048,384]{1,0:T(8,128)(2,1)S(1)} %copy-done.5), kind=kOutput, calls=%fused_computation.27 | convolution fusion | flops 3227516928 | bytes 10485760 | tf_op jit(solution)/shard_map/dot_general | solution.py:8
  73.0 34.1 %all-gather.3.cloned.1.call-done = bf16[1024,2048]{1,0:T(8,128)(2,1)} async-done(((bf16[128,2048]{1,0:T(8,128)(2,1)}), bf16[1024,2048]{1,0:T(8,128)(2,1)}) %all-gather.3.cloned.1.call-update) | async-done | bytes 4194320 | tf_op jit(solution)/shard_map/all_gather | solution.py:26
  107.1 0.0 copy-done
  107.1 0.0 copy-start.10
  107.1 10.6 %multiply_convert_fusion = (bf16[1024,768]{1,0:T(8,128)(2,1)S(1)}, bf16[1024,768]{1,0:T(8,128)(2,1)}) fusion(f32[768,1024]{0,1:T(8,128)} %fusion.12, f32[768,1024]{0,1:T(8,128)} %fusion.13, f32[1024,768]{1,0:T(8,128)} %bitcast.74, bf16[1024,2048]{1,0:T(8,128)(2,1)} %all-gather.3.cloned.1.call-done, bf16[768,2048]{1,0:T(8,128)(2,1)S(1)} %bitcast.72), kind=kOutput, calls=%fused_computation.22 | convolution fusion | flops 3232235520 | bytes 19922944 | tf_op jit(solution)/shard_map/dot_general | solution.py:8
  117.7 0.0 copy-start.11
  117.7 0.0 copy-done.10
  117.7 3.9 %fusion.10 = bf16[2048,768]{0,1:T(8,128)(2,1)S(1)} fusion(bf16[1024,768]{1,0:T(8,128)(2,1)S(1)} %get-tuple-element.12, bf16[1024,2048]{1,0:T(8,128)(2,1)S(1)} %copy-done.10), kind=kOutput, calls=%fused_computation.24 | convolution fusion | flops 3222798336 | bytes 8912896 | tf_op jit(solution)/shard_map/dot_general | solution.py:8
  121.5 0.0 copy-done.11
  121.6 0.2 slice_bitcast_fusion.1
  121.8 2.0 pad_maximum_fusion.3
  123.8 0.0 reduce-scatter.9.cloned.1.call-update
  123.8 0.0 reduce-scatter.7.cloned.1.call-start
  123.8 1.3 copy-done.13
  125.2 5.9 %fusion.9 = bf16[2048,768]{0,1:T(8,128)(2,1)S(1)} fusion(bf16[1024,768]{1,0:T(8,128)(2,1)S(1)} %copy-done.13, bf16[1024,2048]{1,0:T(8,128)(2,1)} %all-gather.5.cloned.1.call-done), kind=kOutput, calls=%fused_computation.23 | convolution fusion | flops 3222798336 | bytes 8912896 | tf_op jit(solution)/shard_map/dot_general | solution.py:8
  131.1 0.2 slice_bitcast_fusion.3
  131.3 2.0 pad_maximum_fusion.2
  133.3 0.0 reduce-scatter.7.cloned.1.call-update
  133.3 0.0 reduce-scatter.11.cloned.1.call-start
  133.3 1.9 copy-done.4
  135.2 9.7 %convolution_convert_fusion = bf16[768,2048]{1,0:T(8,128)(2,1)} fusion(bf16[1024,2048]{1,0:T(8,128)(2,1)} %all-gather.3.cloned.1.call-done, f32[1024,768]{1,0:T(8,128)S(1)} %bitcast.75, f32[768,1024]{0,1:T(8,128)} %fusion.13, f32[768,1024]{0,1:T(8,128)} %fusion.12), kind=kOutput, calls=%fused_computation.1 | convolution fusion | flops 3228303360 | bytes 16777216 | tf_op jit(solution)/shard_map/dot_general | solution.py:8
  144.8 0.0 reduce-scatter.11.cloned.1.call-update
  144.9 0.0 copy-start.6
  144.9 0.0 copy-start.8
  144.9 0.0 reduce-scatter.5.cloned.1.call-start
  144.9 0.0 copy-start.12
  145.0 5.7 %fusion.11 = f32[1024,2048]{1,0:T(8,128)S(1)} fusion(bf16[1024,768]{1,0:T(8,128)(2,1)} %get-tuple-element.13, bf16[2048,384]{1,0:T(8,128)(2,1)} %get-tuple-element.21, bf16[2048,384]{1,0:T(8,128)(2,1)} %get-tuple-element.20), kind=kOutput, calls=%fused_computation.25 | convolution fusion | flops 3227516928 | bytes 13107200 | tf_op jit(solution)/shard_map/dot_general | solution.py:8
  150.7 0.0 copy-done.6
  150.7 0.0 copy-done.8
  150.7 0.0 copy-done.12
  150.7 5.1 %add_convert_fusion = bf16[1024,2048]{1,0:T(8,128)(2,1)} fusion(f32[1024,2048]{1,0:T(8,128)S(1)} %fusion.11, bf16[1024,768]{1,0:T(8,128)(2,1)S(1)} %copy-done.12, bf16[2048,384]{1,0:T(8,128)(2,1)S(1)} %copy-done.8, bf16[2048,384]{1,0:T(8,128)(2,1)S(1)} %copy-done.6), kind=kOutput, calls=%fused_computation | convolution fusion | flops 3231711232 | bytes 17301504 | tf_op jit(solution)/shard_map/dot_general | solution.py:8
  155.8 0.0 reduce-scatter.5.cloned.1.call-update
  155.8 10.8 %reduce-scatter.9.cloned.1.call-done = bf16[2,512,384]{1,2,0:T(8,128)(2,1)} async-done(((bf16[2,2048,384]{1,2,0:T(8,128)(2,1)}), bf16[2,512,384]{1,2,0:T(8,128)(2,1)}) %reduce-scatter.9.cloned.1.call-update) | async-done | bytes 786448 | tf_op jit(solution)/shard_map/reduce_scatter | solution.py:49
  166.6 2.3 copy.21
  168.9 44.5 %reduce-scatter.7.cloned.1.call-done = bf16[2,512,384]{1,2,0:T(8,128)(2,1)} async-done(((bf16[2,2048,384]{1,2,0:T(8,128)(2,1)}), bf16[2,512,384]{1,2,0:T(8,128)(2,1)}) %reduce-scatter.7.cloned.1.call-update) | async-done | bytes 786448 | tf_op jit(solution)/shard_map/reduce_scatter | solution.py:48
  213.4 2.3 copy.20
  215.7 45.1 %reduce-scatter.11.cloned.1.call-done = bf16[2,384,512]{2,1,0:T(8,128)(2,1)} async-done(((bf16[2,384,2048]{2,1,0:T(8,128)(2,1)}), bf16[2,384,512]{2,1,0:T(8,128)(2,1)}) %reduce-scatter.11.cloned.1.call-update) | async-done | bytes 786448 | tf_op jit(solution)/shard_map/reduce_scatter | solution.py:47
  260.8 52.7 %reduce-scatter.5.cloned.1.call-done = bf16[128,2048]{1,0:T(8,128)(2,1)} async-done(((bf16[1024,2048]{1,0:T(8,128)(2,1)}), bf16[128,2048]{1,0:T(8,128)(2,1)}) %reduce-scatter.5.cloned.1.call-update) | async-done | bytes 524304 | tf_op jit(solution)/shard_map/reduce_scatter | solution.py:46
  313.5 0.0 copy-done.1
  (4 shorter events, 0.0 us)
Async XLA Ops:
  7.2 99.9 %copy-start = (bf16[2,384,2048]{2,1,0:T(8,128)(2,1)S(1)}, bf16[2,384,2048]{2,1,0:T(8,128)(2,1)}, u32[]{:S(2)}) copy-start(bf16[2,384,2048]{2,1,0:T(8,128)(2,1)} %param.13) | copy-start | bytes 9437188
  7.2 52.4 %all-gather.5.cloned.1.call-start = ((), (), s32[]{:S(2)}) async-start(), calls=%async_computation.5 | async-start | bytes 4718592 | tf_op jit(solution)/shard_map/all_gather | solution.py:25
  7.9 99.1 %all-gather.3.cloned.1.call-start = ((), (), s32[]{:S(2)}) async-start(), calls=%async_computation.4 | async-start | bytes 4718592 | tf_op jit(solution)/shard_map/all_gather | solution.py:26
  8.7 158.0 %reduce-scatter.9.cloned.1.call-start = ((), (), s32[]{:S(2)}) async-start(), calls=%async_computation.8 | async-start | bytes 3932160 | tf_op jit(solution)/shard_map/reduce_scatter | solution.py:49
  29.3 3.0 copy-start.2
  32.4 3.0 copy-start.3
  59.6 8.3 %copy-start.5 = (bf16[2048,384]{1,0:T(8,128)(2,1)S(1)}, bf16[2048,384]{1,0:T(8,128)(2,1)}, u32[]{:S(2)}) copy-start(bf16[2048,384]{1,0:T(8,128)(2,1)} %get-tuple-element.18) | copy-start | bytes 4718596
  59.6 8.3 %copy-start.7 = (bf16[2048,384]{1,0:T(8,128)(2,1)S(1)}, bf16[2048,384]{1,0:T(8,128)(2,1)}, u32[]{:S(2)}) copy-start(bf16[2048,384]{1,0:T(8,128)(2,1)} %get-tuple-element.19) | copy-start | bytes 4718596
  59.6 8.3 %copy-start.9 = (bf16[1024,2048]{1,0:T(8,128)(2,1)S(1)}, bf16[1024,2048]{1,0:T(8,128)(2,1)}, u32[]{:S(2)}) copy-start(bf16[1024,2048]{1,0:T(8,128)(2,1)} %all-gather.5.cloned.1.call-done) | copy-start | bytes 12582916
  107.1 10.6 %copy-start.10 = (bf16[1024,2048]{1,0:T(8,128)(2,1)S(1)}, bf16[1024,2048]{1,0:T(8,128)(2,1)}, u32[]{:S(2)}) copy-start(bf16[1024,2048]{1,0:T(8,128)(2,1)} %all-gather.5.cloned.1.call-done) | copy-start | bytes 12582916
  117.7 3.9 %copy-start.11 = (bf16[1024,768]{1,0:T(8,128)(2,1)}, bf16[1024,768]{1,0:T(8,128)(2,1)S(1)}, u32[]{:S(2)}) copy-start(bf16[1024,768]{1,0:T(8,128)(2,1)S(1)} %get-tuple-element.12) | copy-start | bytes 4718596
  123.8 1.4 copy-start.13
  123.8 89.6 %reduce-scatter.7.cloned.1.call-start = ((), (), s32[]{:S(2)}) async-start(), calls=%async_computation.7 | async-start | bytes 3932160 | tf_op jit(solution)/shard_map/reduce_scatter | solution.py:48
  133.3 1.9 copy-start.4
  133.3 127.5 %reduce-scatter.11.cloned.1.call-start = ((), (), s32[]{:S(2)}) async-start(), calls=%async_computation.9 | async-start | bytes 3932160 | tf_op jit(solution)/shard_map/reduce_scatter | solution.py:47
  144.9 5.8 %copy-start.6 = (bf16[2048,384]{1,0:T(8,128)(2,1)S(1)}, bf16[2048,384]{1,0:T(8,128)(2,1)}, u32[]{:S(2)}) copy-start(bf16[2048,384]{1,0:T(8,128)(2,1)} %get-tuple-element.18) | copy-start | bytes 4718596
  144.9 5.8 %copy-start.8 = (bf16[2048,384]{1,0:T(8,128)(2,1)S(1)}, bf16[2048,384]{1,0:T(8,128)(2,1)}, u32[]{:S(2)}) copy-start(bf16[2048,384]{1,0:T(8,128)(2,1)} %get-tuple-element.19) | copy-start | bytes 4718596
  144.9 168.7 %reduce-scatter.5.cloned.1.call-start = ((), (), s32[]{:S(2)}) async-start(), calls=%async_computation.6 | async-start | bytes 4718592 | tf_op jit(solution)/shard_map/reduce_scatter | solution.py:46
  144.9 5.8 %copy-start.12 = (bf16[1024,768]{1,0:T(8,128)(2,1)S(1)}, bf16[1024,768]{1,0:T(8,128)(2,1)}, u32[]{:S(2)}) copy-start(bf16[1024,768]{1,0:T(8,128)(2,1)} %copy-done.11) | copy-start | bytes 4718596
  155.8 157.8 %copy-start.1 = (bf16[2,384,2048]{2,1,0:T(8,128)(2,1)S(1)}, bf16[2,384,2048]{2,1,0:T(8,128)(2,1)}, u32[]{:S(2)}) copy-start(bf16[2,384,2048]{2,1,0:T(8,128)(2,1)} %param.13) | copy-start | bytes 9437188
Sparse Core Ops, SparseCore 0:
  9.6 49.9 all-gather.4
  61.2 45.8 all-gather.2
  123.9 42.6 reduce-scatter.8
  169.5 43.9 reduce-scatter.6
  216.8 43.9 reduce-scatter.10
  263.5 49.9 reduce-scatter.4

commit v2 on v1

--- a/solution.py
+++ b/solution.py
@@ -1,6 +1,10 @@
+import functools
+
 import jax
 import jax.numpy as jnp
 from jax import lax
+from jax.experimental import pallas as pl
+from jax.experimental.pallas import tpu as pltpu
 from jax.sharding import PartitionSpec as P
 
 
@@ -8,6 +12,208 @@
     return lax.dot_general(
         left, right, (((left_dim,), (right_dim,)), ((), ())), preferred_element_type=jnp.float32
     )
+
+
+MESH = pl.DeviceIdType.MESH
+
+
+def ring_owner(place, n):
+    return jnp.where(place < n // 2, 2 * place, 2 * (n - 1 - place) + 1)
+
+
+def reduce_kernel(
+    n, xt_ref, dy_ref, dgu_ref, actt_ref, w_ref,
+    in_ref, out_gu, out_d,
+    g_gu, g_d, r1_gu, r1_d, r2_gu, r2_d, part, landed,
+    s1_send, s1_recv, s2_send, s2_recv, ring_send, ring_recv,
+):
+    f32, bf16 = jnp.float32, jnp.bfloat16
+    me = lax.axis_index("dp")
+    q = lax.axis_index("expert")
+    xx, yy = me % 2, me // 2
+    xn = yy * 2 + (1 - xx)
+    yn = (1 - yy) * 2 + xx
+    diag = 3 - me
+    place = jnp.where(q % 2 == 0, q // 2, n - 1 - q // 2)
+    right = ring_owner((place + 1) % n, n)
+    left = ring_owner((place + n - 1) % n, n)
+
+    barrier = pltpu.get_barrier_semaphore()
+    for target in ((xn, q), (yn, q), (me, right), (me, left)):
+        pl.semaphore_signal(barrier, inc=1, device_id=target, device_id_type=MESH)
+    pl.semaphore_wait(barrier, 4)
+
+    gu_rows, gu_cols = g_gu.shape[2:]
+    d_rows, d_cols = g_d.shape[2:]
+    tile = 512
+
+    def weight_grads(block, half):
+        rows = pl.multiple_of((block * 2 + half) * gu_rows, gu_rows)
+
+        def step(i, carry):
+            cols = pl.ds(pl.multiple_of(i * tile, tile), tile)
+            g_gu[block, half, :, cols] = jnp.dot(
+                xt_ref[pl.ds(rows, gu_rows), :], dgu_ref[:, cols], preferred_element_type=f32
+            ).astype(bf16)
+            return carry
+
+        lax.fori_loop(0, gu_cols // tile, step, 0)
+        g_d[block, half] = jnp.dot(
+            actt_ref[pl.ds(half * d_rows, d_rows), :],
+            dy_ref[:, pl.ds(pl.multiple_of(block * d_cols, d_cols), d_cols)],
+            preferred_element_type=f32,
+        ).astype(bf16)
+
+    def first(block, half, slot):
+        target = (xn, q) if half == 0 else (yn, q)
+        copies = []
+        for kind, (src, dst) in enumerate(((g_gu, r1_gu), (g_d, r1_d))):
+            copies.append(pltpu.make_async_remote_copy(
+                src_ref=src.at[block, half], dst_ref=dst.at[half, slot],
+                send_sem=s1_send.at[half, slot, kind], recv_sem=s1_recv.at[half, slot, kind],
+                device_id=target, device_id_type=MESH))
+        return copies
+
+    def second(block, half):
+        target = (yn, q) if half == 0 else (xn, q)
+        copies = []
+        for kind, (src, dst) in enumerate(((g_gu, r2_gu), (g_d, r2_d))):
+            copies.append(pltpu.make_async_remote_copy(
+                src_ref=src.at[block, half], dst_ref=dst.at[half],
+                send_sem=s2_send.at[half, kind], recv_sem=s2_recv.at[half, kind],
+                device_id=target, device_id_type=MESH))
+        return copies
+
+    tok = in_ref.shape[0]
+    hrow = tok // 2
+
+    def ring_rows(s, way):
+        if way == 0:
+            owner = ring_owner((place + 2 * n - 1 - s) % n, n)
+        else:
+            owner = ring_owner((place + 1 + s) % n, n)
+        return pl.ds(pl.multiple_of(owner * tok + way * hrow, hrow), hrow)
+
+    def ring_copy(s, way):
+        return pltpu.make_async_remote_copy(
+            src_ref=part.at[ring_rows(s, way)], dst_ref=landed.at[way, s],
+            send_sem=ring_send.at[way, s], recv_sem=ring_recv.at[way, s],
+            device_id=(me, right if way == 0 else left), device_id_type=MESH)
+
+    def ring_step(s):
+        for way in range(2):
+            if s > 0:
+                ring_copy(s - 1, way).wait_recv()
+                rows = ring_rows(s, way)
+                part[rows] = (part[rows].astype(f32) + landed[way, s - 1].astype(f32)).astype(bf16)
+            ring_copy(s, way).start()
+
+    sends = []
+
+    def go(copies):
+        for copy in copies:
+            copy.start()
+        sends.extend(copies)
+
+    weight_grads(diag, 0)
+    first0 = first(diag, 0, 0)
+    go(first0)
+    weight_grads(diag, 1)
+    first1 = first(diag, 1, 0)
+    go(first1)
+
+    band = 256
+
+    def contrib(i, carry):
+        rows = pl.ds(pl.multiple_of((i // 4) * band, band), band)
+        cols = pl.ds(pl.multiple_of((i % 4) * tile, tile), tile)
+        part[rows, cols] = lax.dot_general(
+            dgu_ref[rows, :], w_ref[cols, :], (((1,), (1,)), ((), ())), preferred_element_type=f32
+        ).astype(bf16)
+        return carry
+
+    lax.fori_loop(0, part.shape[0] // band * 4, contrib, 0)
+    ring_step(0)
+    weight_grads(xn, 0)
+    keep0 = first(xn, 0, 1)
+    go(keep0)
+    weight_grads(yn, 1)
+    keep1 = first(yn, 1, 1)
+    go(keep1)
+    ring_step(1)
+    weight_grads(yn, 0)
+    weight_grads(xn, 1)
+    ring_step(2)
+    for half, (block, copies) in enumerate(((yn, first0), (xn, first1))):
+        copies[0].wait_recv()
+        copies[1].wait_recv()
+        g_gu[block, half] = (g_gu[block, half].astype(f32) + r1_gu[half, 0].astype(f32)).astype(bf16)
+        g_d[block, half] = (g_d[block, half].astype(f32) + r1_d[half, 0].astype(f32)).astype(bf16)
+        go(second(block, half))
+    ring_step(3)
+    weight_grads(me, 0)
+    ring_step(4)
+    weight_grads(me, 1)
+    for s in range(5, n - 1):
+        ring_step(s)
+    for way in range(2):
+        ring_copy(n - 2, way).wait_recv()
+        rows = pl.ds(pl.multiple_of(q * tok + way * hrow, hrow), hrow)
+        in_ref[pl.ds(way * hrow, hrow), :] = (
+            part[rows].astype(f32) + landed[way, n - 2].astype(f32)).astype(bf16)
+    for half, copies in enumerate((keep0, keep1)):
+        copies[0].wait_recv()
+        copies[1].wait_recv()
+        last = second(yn if half == 0 else xn, half)
+        last[0].wait_recv()
+        out_gu[half] = (g_gu[me, half].astype(f32) + r1_gu[half, 1].astype(f32)
+                        + r2_gu[half].astype(f32)).astype(bf16)
+        last[1].wait_recv()
+        out_d[half] = (g_d[me, half].astype(f32) + r1_d[half, 1].astype(f32)
+                       + r2_d[half].astype(f32)).astype(bf16)
+    for copy in sends:
+        copy.wait_send()
+    for s in range(n - 1):
+        for way in range(2):
+            ring_copy(s, way).wait_send()
+
+
+def reduce_call(xt, dy, dgu, actt, w_gu, n, tok):
+    bf16 = jnp.bfloat16
+    width, total = xt.shape
+    gu = dgu.shape[1]
+    hid = actt.shape[0]
+    rows, cols = width // 8, width // 4
+    vmem = pl.BlockSpec(memory_space=pltpu.VMEM)
+    return pl.pallas_call(
+        functools.partial(reduce_kernel, n),
+        out_shape=(
+            jax.ShapeDtypeStruct((tok, width), bf16),
+            jax.ShapeDtypeStruct((2, rows, gu), bf16),
+            jax.ShapeDtypeStruct((2, hid // 2, cols), bf16),
+        ),
+        in_specs=[vmem] * 5,
+        out_specs=(vmem,) * 3,
+        scratch_shapes=[
+            pltpu.VMEM((4, 2, rows, gu), bf16),
+            pltpu.VMEM((4, 2, hid // 2, cols), bf16),
+            pltpu.VMEM((2, 2, rows, gu), bf16),
+            pltpu.VMEM((2, 2, hid // 2, cols), bf16),
+            pltpu.VMEM((2, rows, gu), bf16),
+            pltpu.VMEM((2, hid // 2, cols), bf16),
+            pltpu.VMEM((total, width), bf16),
+            pltpu.VMEM((2, n - 1, tok // 2, width), bf16),
+            pltpu.SemaphoreType.DMA((2, 2, 2)),
+            pltpu.SemaphoreType.DMA((2, 2, 2)),
+            pltpu.SemaphoreType.DMA((2, 2)),
+            pltpu.SemaphoreType.DMA((2, 2)),
+            pltpu.SemaphoreType.DMA((2, n - 1)),
+            pltpu.SemaphoreType.DMA((2, n - 1)),
+        ],
+        compiler_params=pltpu.CompilerParams(
+            collective_id=0, has_side_effects=True, vmem_limit_bytes=60 * 1024 * 1024
+        ),
+    )(xt, dy, dgu, actt, w_gu)
 
 
 def per_device(tokens, out_grad, expert_ids, route_probs, gate_weight, up_weight, down_weight):
@@ -37,6 +243,14 @@
     act = (silu * up * prob).astype(bf16)
     dgate = (dh * slope).astype(bf16)
     dup = (dh * silu).astype(bf16)
+    if exp_dev == 2 and lax.axis_size("dp") == 4 and n_owner == 8:
+        in_grad, gu, down = reduce_call(
+            x.T, dy, jnp.concatenate([dgate, dup], axis=1), act.T,
+            jnp.concatenate([w_gate, w_up], axis=1), n_owner, tokens.shape[0],
+        )
+        gu = gu.reshape(width // 4, 2, exp_dev, hid)
+        grad_g, grad_u = (gu[:, k].transpose(1, 0, 2) for k in range(2))
+        return (in_grad, grad_g, grad_u, down)
     grad_d = contract(act, dy, 0, 0).astype(bf16).reshape(exp_dev, hid, width)
     grad_g = contract(x, dgate, 0, 0).astype(bf16)
     grad_u = contract(x, dup, 0, 0).astype(bf16)

time: 321 us -> 236 us (0.74)
  waiting for transfers between devices: 211 us -> 64.9 us
  Pallas kernels: 0 us -> 92.6 us
  matrix products: 54.2 us -> 20 us
    reduce_scatter x4 -> x0, waiting for transfers between devices: 153 us -> none  [the longest x1 52.7 us: per_device(): in_grad = lax.psum_scatter(part, 'expert', scatter_dimension=0, tiled=True)]
    pallas_call x0 -> x1, Pallas kernels: none -> 92.6 us  [reduce_call(): pl.pallas_call(functools.partial(reduce_kernel, n), out_shape=(jax.ShapeD...]
    dot_general x8 -> x3, matrix products: 54.2 us -> 20 us  [contract(): lax.dot_general(left, right, (((left_dim,), (right_dim,)), ((), ())), pre...]
    unnamed x31 -> x27, local copies, waits for them, and re-layouts: 11.8 us -> 6.77 us
    concatenate x0 -> x2, other arithmetic: none -> 5.03 us  [the longest x1 3.1 us: per_device(): jnp.concatenate([w_gate, w_up], axis=1)]
    concatenate x0 -> x1, local copies, waits for them, and re-layouts: none -> 4.67 us  [per_device(): jnp.concatenate([dgate, dup], axis=1)]
    all_gather x1, waiting for transfers between devices: 34.1 us -> 38.8 us  [per_device(): dy = lax.all_gather(out_grad, 'expert', axis=0, tiled=True)]
    reshape x0 -> x1, local copies, waits for them, and re-layouts: none -> 4.57 us  [per_device(): gu = gu.reshape(width // 4, 2, exp_dev, hid)]
  transfers between devices with their start and end apart: 6 -> 2, of which waited for: 6 -> 2; matrix products, arithmetic and copies ran while one was open for 18% -> 6% of each run, Pallas kernels for 0% -> 0%
where the time goes in v2:
time: 236 us
  Pallas kernels  92.6 us (39%)
  waiting for transfers between devices  64.9 us (28%)
  local copies, waits for them, and re-layouts  22.6 us (10%)
  matrix products  20 us (8%)
  blocking collectives  15.7 us (7%)
  between operations  14.1 us (6%)
  other arithmetic  5.75 us (2%)
    pallas_call x1, Pallas kernels, reduce_call(): pl.pallas_call(functools.partial(reduce_kernel, n), out_shape=(jax.ShapeD...  92.6 us
    all_gather x1, waiting for transfers between devices, per_device(): dy = lax.all_gather(out_grad, 'expert', axis=0, tiled=True)  38.8 us
    all_gather x1, waiting for transfers between devices, per_device(): x = lax.all_gather(tokens, 'expert', axis=0, tiled=True)  25.4 us
    dot_general x3, matrix products, contract(): lax.dot_general(left, right, (((left_dim,), (right_dim,)), ((), ())), pre...  20 us
    all_gather x1, blocking collectives, per_device(): all_weight = lax.all_gather(weight, 'expert', axis=0, tiled=True)  15.7 us
    unnamed x27, local copies, waits for them, and re-layouts  6.77 us
  transfers between devices with their start and end apart: 2, of which 2 were waited for; matrix products, arithmetic and copies ran while one was open for 6% of the time, Pallas kernels for 0%

profile of v2, /device:TPU:0, one launch (start us, length us, event | category | flops | bytes accessed | tf_op | source)
XLA Modules:
  0.0 235.8 jit_solution(8842294559017918290)
XLA Ops:
  7.2 0.0 copy-start
  7.2 0.0 all-gather.3.cloned.1.call-start
  7.2 2.2 copy.17
  9.4 0.0 all-gather.3.cloned.1.call-update
  9.4 0.0 all-gather.5.cloned.1.call-start
  9.5 0.7 all-gather.5.cloned.1.call-update
  10.2 0.7 select_reduce_fusion
  10.9 15.7 %all_gather.11 = f32[1024,16]{0,1:T(8,128)S(1)} all-gather(f32[128,16]{0,1:T(8,128)S(1)} %select_reduce_fusion), channel_id=1, replica_groups=mesh['dp'=4,'expert'=8] {'expert'}, dimensions={0}, use_global_device_ids=true | all-gather | bytes 73728 | tf_op jit(solution)/shard_map/all_gather | solution.py:229
  26.7 0.0 copy-start.8
  26.7 2.3 slice_bitcast_fusion.1
  29.0 0.5 copy-done.8
  29.5 0.0 copy-start.6
  29.5 0.0 copy-start.7
  29.5 0.3 slice_bitcast_fusion.3
  29.8 0.0 copy-start.2
  29.8 0.0 copy-start.4
  29.8 0.8 copy-done.6
  30.7 0.5 copy-done.7
  31.2 0.6 copy-done.2
  31.7 0.5 copy-done.4
  32.2 3.1 %pad_maximum_fusion.w_ref = bf16[2048,1536]{1,0:T(8,128)(2,1)} fusion(bf16[2048,384]{1,0:T(8,128)(2,1)S(1)} %get-tuple-element.14, bf16[2048,384]{1,0:T(8,128)(2,1)S(1)} %get-tuple-element.13, bf16[2048,384]{1,0:T(8,128)(2,1)S(1)} %get-tuple-element.16, bf16[2048,384]{1,0:T(8,128)(2,1)S(1)} %get-tuple-element.15), kind=kLoop, calls=%fused_computation | loop fusion | flops 25165824 | bytes 12582912 | tf_op jit(solution)/shard_map/concatenate | solution.py:249
  35.3 25.4 %all-gather.3.cloned.1.call-done = bf16[1024,2048]{0,1:T(8,128)(2,1)} async-done(((bf16[128,2048]{0,1:T(8,128)(2,1)}), bf16[1024,2048]{0,1:T(8,128)(2,1)}) %all-gather.3.cloned.1.call-update) | async-done | bytes 4194320 | tf_op jit(solution)/shard_map/all_gather | solution.py:231
  60.8 8.2 %fusion.5 = f32[768,1024]{1,0:T(8,128)} fusion(bf16[1024,2048]{0,1:T(8,128)(2,1)} %all-gather.3.cloned.1.call-done, bf16[2048,384]{1,0:T(8,128)(2,1)} %copy-done.7, bf16[2048,384]{1,0:T(8,128)(2,1)} %copy-done.6), kind=kOutput, calls=%fused_computation.8 | convolution fusion | flops 3227516928 | bytes 10485760 | tf_op jit(solution)/shard_map/dot_general | solution.py:12
  69.0 38.8 %all-gather.5.cloned.1.call-done.dy_ref = bf16[1024,2048]{1,0:T(8,128)(2,1)} async-done(((bf16[128,2048]{1,0:T(8,128)(2,1)}), bf16[1024,2048]{1,0:T(8,128)(2,1)}) %all-gather.5.cloned.1.call-update) | async-done | bytes 4194320 | tf_op jit(solution)/shard_map/all_gather | solution.py:232
  107.8 0.0 copy-done
  107.8 0.0 copy-start.1
  107.8 0.0 copy-start.3
  107.8 0.0 copy-start.5
  107.8 0.0 copy-start.9
  107.8 5.4 %fusion.19 = f32[1024,768]{0,1:T(8,128)S(1)} fusion(bf16[1024,2048]{1,0:T(8,128)(2,1)} %all-gather.5.cloned.1.call-done.dy_ref, bf16[768,2048]{1,0:T(8,128)(2,1)S(1)} %bitcast.65), kind=kOutput, calls=%fused_computation.38 | convolution fusion | flops 3221225472 | bytes 10485760 | tf_op jit(solution)/shard_map/dot_general | solution.py:12
  113.2 0.0 copy-done.1
  113.2 0.0 copy-done.3
  113.2 0.0 copy-done.5
  113.2 0.0 copy-done.9
  113.2 6.4 %fusion = (bf16[1024,768]{0,1:T(8,128)(2,1)}, bf16[1024,768]{0,1:T(8,128)(2,1)S(1)}, bf16[1024,768]{0,1:T(8,128)(2,1)S(1)}) fusion(f32[1024,2]{0,1:T(2,128)S(1)} %constant_dynamic-slice_fusion, f32[768,1024]{1,0:T(8,128)S(1)} %copy-done.9, f32[1024,768]{0,1:T(8,128)S(1)} %fusion.19, bf16[1024,2048]{0,1:T(8,128)(2,1)S(1)} %copy-done.1, ...), kind=kOutput, calls=%fused_computation.3 | convolution fusion | flops 3240886272 | bytes 18358272 | tf_op jit(solution)/shard_map/dot_general | solution.py:12
  119.6 1.9 pad_maximum_fusion.1
  121.5 4.7 %copy.18.dgu_ref = bf16[1024,1536]{1,0:T(8,128)(2,1)} copy(bf16[1024,1536]{0,1:T(8,128)(2,1)} %pad_maximum_fusion.1) | data formatting | bytes 6291456 | tf_op jit(solution)/shard_map/concatenate | solution.py:248
  126.2 92.6 %shard_map.102 = (bf16[128,2048]{1,0:T(8,128)(2,1)}, bf16[2,256,1536]{2,1,0:T(8,128)(2,1)}, bf16[2,384,512]{2,1,0:T(8,128)(2,1)}) custom-call(bf16[2048,1024]{1,0:T(8,128)(2,1)} %bitcast.66, bf16[1024,2048]{1,0:T(8,128)(2,1)} %all-gather.5.cloned.1.call-done.dy_ref, bf16[1024,1536]{1,0:T(8,128)(2,1)} %copy.18.dgu_ref, bf16[768,1024]{1,0:T(8,128)(2,1)} %bitcast.67, ...), custom_call_target="tpu_custom_call" | custom-call | tf_op jit(solution)/shard_map/pallas_call | solution.py:188
  218.8 4.6 %reshape.21 = bf16[512,2,2,384]{3,2,1,0:T(2,128)(2,1)} reshape(bf16[2,256,1536]{2,1,0:T(8,128)(2,1)} %get-tuple-element.8) | data formatting | bytes 3145728 | tf_op jit(solution)/shard_map/reshape | solution.py:251
  223.4 0.0 copy-start.11
  223.4 0.0 copy-start.10
  223.4 2.6 %fusion.18 = (bf16[512,1,2,384]{3,2,1,0:T(2,128)(2,1)S(1)}, bf16[512,1,2,384]{3,2,1,0:T(2,128)(2,1)S(1)}) fusion(bf16[512,2,2,384]{3,2,1,0:T(2,128)(2,1)} %reshape.21), kind=kLoop, calls=%fused_computation.37 | loop fusion | bytes 3145728 | tf_op jit(solution)/shard_map/slice | solution.py:252
  225.9 1.3 copy_bitcast_fusion
  227.3 0.0 copy-done.11
  227.3 0.8 copy.27
  228.1 0.0 copy-done.10
  228.1 0.9 copy.28
  (1 shorter events, 0.0 us)
Async XLA Ops:
  7.2 100.6 %copy-start = (bf16[2,384,2048]{2,1,0:T(8,128)(2,1)S(1)}, bf16[2,384,2048]{2,1,0:T(8,128)(2,1)}, u32[]{:S(2)}) copy-start(bf16[2,384,2048]{2,1,0:T(8,128)(2,1)} %param.13) | copy-start | bytes 9437188
  7.2 53.6 %all-gather.3.cloned.1.call-start = ((), (), s32[]{:S(2)}) async-start(), calls=%async_computation | async-start | bytes 4718592 | tf_op jit(solution)/shard_map/all_gather | solution.py:231
  9.4 98.3 %all-gather.5.cloned.1.call-start = ((), (), s32[]{:S(2)}) async-start(), calls=%async_computation.1 | async-start | bytes 4718592 | tf_op jit(solution)/shard_map/all_gather | solution.py:232
  26.7 2.8 %copy-start.8 = (bf16[2,2048,384]{2,1,0:T(8,128)(2,1)S(1)}, bf16[2,2048,384]{2,1,0:T(8,128)(2,1)}, u32[]{:S(2)}) copy-start(bf16[2,2048,384]{2,1,0:T(8,128)(2,1)} %param.12) | copy-start | bytes 9437188
  29.5 1.1 copy-start.6
  29.5 1.7 copy-start.7
  29.8 1.9 copy-start.2
  29.8 2.4 %copy-start.4 = (bf16[2048,384]{1,0:T(8,128)(2,1)}, bf16[2048,384]{1,0:T(8,128)(2,1)S(1)}, u32[]{:S(2)}) copy-start(bf16[2048,384]{1,0:T(8,128)(2,1)S(1)} %get-tuple-element.14) | copy-start | bytes 4718596
  107.8 5.4 %copy-start.1 = (bf16[1024,2048]{0,1:T(8,128)(2,1)S(1)}, bf16[1024,2048]{0,1:T(8,128)(2,1)}, u32[]{:S(2)}) copy-start(bf16[1024,2048]{0,1:T(8,128)(2,1)} %all-gather.3.cloned.1.call-done) | copy-start | bytes 12582916
  107.8 5.4 %copy-start.3 = (bf16[2048,384]{1,0:T(8,128)(2,1)S(1)}, bf16[2048,384]{1,0:T(8,128)(2,1)}, u32[]{:S(2)}) copy-start(bf16[2048,384]{1,0:T(8,128)(2,1)} %copy-done.2) | copy-start | bytes 4718596
  107.8 5.5 %copy-start.5 = (bf16[2048,384]{1,0:T(8,128)(2,1)S(1)}, bf16[2048,384]{1,0:T(8,128)(2,1)}, u32[]{:S(2)}) copy-start(bf16[2048,384]{1,0:T(8,128)(2,1)} %copy-done.4) | copy-start | bytes 4718596
  107.8 5.5 %copy-start.9 = (f32[768,1024]{1,0:T(8,128)S(1)}, f32[768,1024]{1,0:T(8,128)}, u32[]{:S(2)}) copy-start(f32[768,1024]{1,0:T(8,128)} %fusion.5) | copy-start | bytes 9437188
  223.4 3.9 %copy-start.11 = (bf16[128,2048]{1,0:T(8,128)(2,1)S(1)}, bf16[128,2048]{1,0:T(8,128)(2,1)}, u32[]{:S(2)}) copy-start(bf16[128,2048]{1,0:T(8,128)(2,1)} %get-tuple-element.25) | copy-start | bytes 1572868
  223.4 4.7 %copy-start.10 = (bf16[2,384,512]{2,1,0:T(8,128)(2,1)S(1)}, bf16[2,384,512]{2,1,0:T(8,128)(2,1)}, u32[]{:S(2)}) copy-start(bf16[2,384,512]{2,1,0:T(8,128)(2,1)} %get-tuple-element.28) | copy-start | bytes 2359300
Sparse Core Ops, SparseCore 0:
  10.2 50.5 all-gather.2
  62.4 45.3 all-gather.4

commit v3 on v2

--- a/solution.py
+++ b/solution.py
@@ -23,7 +23,7 @@
 
 def reduce_kernel(
     n, xt_ref, dy_ref, dgu_ref, actt_ref, w_ref,
-    in_ref, out_gu, out_d,
+    in_ref, out_g, out_u, out_d,
     g_gu, g_d, r1_gu, r1_d, r2_gu, r2_d, part, landed,
     s1_send, s1_recv, s2_send, s2_recv, ring_send, ring_recv,
 ):
@@ -166,8 +166,13 @@
         copies[1].wait_recv()
         last = second(yn if half == 0 else xn, half)
         last[0].wait_recv()
-        out_gu[half] = (g_gu[me, half].astype(f32) + r1_gu[half, 1].astype(f32)
-                        + r2_gu[half].astype(f32)).astype(bf16)
+        whole = (g_gu[me, half].astype(f32) + r1_gu[half, 1].astype(f32)
+                 + r2_gu[half].astype(f32)).astype(bf16)
+        hid = out_g.shape[2]
+        for e in range(2):
+            rows = slice(half * gu_rows, (half + 1) * gu_rows)
+            out_g[e, rows, :] = whole[:, e * hid:(e + 1) * hid]
+            out_u[e, rows, :] = whole[:, (2 + e) * hid:(3 + e) * hid]
         last[1].wait_recv()
         out_d[half] = (g_d[me, half].astype(f32) + r1_d[half, 1].astype(f32)
                        + r2_d[half].astype(f32)).astype(bf16)
@@ -189,11 +194,12 @@
         functools.partial(reduce_kernel, n),
         out_shape=(
             jax.ShapeDtypeStruct((tok, width), bf16),
-            jax.ShapeDtypeStruct((2, rows, gu), bf16),
+            jax.ShapeDtypeStruct((2, 2 * rows, gu // 4), bf16),
+            jax.ShapeDtypeStruct((2, 2 * rows, gu // 4), bf16),
             jax.ShapeDtypeStruct((2, hid // 2, cols), bf16),
         ),
         in_specs=[vmem] * 5,
-        out_specs=(vmem,) * 3,
+        out_specs=(vmem,) * 4,
         scratch_shapes=[
             pltpu.VMEM((4, 2, rows, gu), bf16),
             pltpu.VMEM((4, 2, hid // 2, cols), bf16),
@@ -216,6 +222,116 @@
     )(xt, dy, dgu, actt, w_gu)
 
 
+def gather_kernel(
+    n, tok_ref, own_dy_ref, own_wt_ref, w_ref, wd_ref,
+    x_ref, dy_ref, dgu_ref, act_ref, wt_ref, send, recv,
+):
+    f32, bf16 = jnp.float32, jnp.bfloat16
+    me = lax.axis_index("dp")
+    q = lax.axis_index("expert")
+    place = jnp.where(q % 2 == 0, q // 2, n - 1 - q // 2)
+    right = ring_owner((place + 1) % n, n)
+    left = ring_owner((place + n - 1) % n, n)
+    tok = tok_ref.shape[0]
+    hrow = tok // 2
+    hid = wd_ref.shape[0] // 2
+    arrays = (x_ref, dy_ref, wt_ref)
+
+    own = pl.ds(pl.multiple_of(q * tok, tok), tok)
+    x_ref[own, :] = tok_ref[...]
+    dy_ref[own, :] = own_dy_ref[...]
+    wt_ref[own, :] = own_wt_ref[...]
+
+    barrier = pltpu.get_barrier_semaphore()
+    for target in ((me, right), (me, left)):
+        pl.semaphore_signal(barrier, inc=1, device_id=target, device_id_type=MESH)
+    pl.semaphore_wait(barrier, 2)
+
+    def rows_of(s, way):
+        owner = ring_owner((place + n - s) % n if way == 0 else (place + s) % n, n)
+        return pl.ds(pl.multiple_of(owner * tok + way * hrow, hrow), hrow)
+
+    def copy(kind, s, way, slot):
+        rows = rows_of(s, way)
+        return pltpu.make_async_remote_copy(
+            src_ref=arrays[kind].at[rows], dst_ref=arrays[kind].at[rows],
+            send_sem=send.at[way, slot, kind], recv_sem=recv.at[way, slot, kind],
+            device_id=(me, right if way == 0 else left), device_id_type=MESH)
+
+    def step(s, carry):
+        @pl.when(s > 0)
+        def _():
+            for kind in range(3):
+                for way in range(2):
+                    copy(kind, s, way, s - 1).wait_recv()
+
+        @pl.when(s < n - 1)
+        def _():
+            for kind in range(3):
+                for way in range(2):
+                    copy(kind, s, way, s).start()
+
+        first, second = rows_of(s, 0), rows_of(s, 1)
+        xb = jnp.concatenate([x_ref[first, :], x_ref[second, :]], axis=0)
+        dyb = jnp.concatenate([dy_ref[first, :], dy_ref[second, :]], axis=0)
+        wt = jnp.concatenate([wt_ref[first, :], wt_ref[second, :]], axis=0)
+        lane = lax.broadcasted_iota(jnp.int32, wt.shape, 1)
+        for e in range(2):
+            prob = jnp.sum(jnp.where(lane == 2 * q + e, wt, 0.0), axis=1, keepdims=True)
+            lo, hi = e * hid, (e + 1) * hid
+            gate = jnp.dot(xb, w_ref[:, lo:hi], preferred_element_type=f32)
+            up = jnp.dot(xb, w_ref[:, 2 * hid + lo:2 * hid + hi], preferred_element_type=f32)
+            dh = prob * lax.dot_general(
+                dyb, wd_ref[lo:hi, :], (((1,), (1,)), ((), ())), preferred_element_type=f32)
+            sig = jax.nn.sigmoid(gate)
+            silu = gate * sig
+            act = (silu * up * prob).astype(bf16)
+            dgate = (dh * up * sig * (1.0 + gate * (1.0 - sig))).astype(bf16)
+            dup = (dh * silu).astype(bf16)
+            for rows, a in ((first, 0), (second, hrow)):
+                act_ref[rows, lo:hi] = act[a:a + hrow]
+                dgu_ref[rows, lo:hi] = dgate[a:a + hrow]
+                dgu_ref[rows, 2 * hid + lo:2 * hid + hi] = dup[a:a + hrow]
+        return carry
+
+    lax.fori_loop(0, n, step, 0)
+
+    def drain(s, carry):
+        for kind in range(3):
+            for way in range(2):
+                copy(kind, s, way, s).wait_send()
+        return carry
+
+    lax.fori_loop(0, n - 1, drain, 0)
+
+
+def gather_call(tokens, out_grad, weight, w_gu, w_down, n):
+    bf16 = jnp.bfloat16
+    tok, width = tokens.shape
+    total = n * tok
+    weight = jnp.pad(weight, ((0, 0), (0, 128 - weight.shape[1])))
+    vmem = pl.BlockSpec(memory_space=pltpu.VMEM)
+    return pl.pallas_call(
+        functools.partial(gather_kernel, n),
+        out_shape=(
+            jax.ShapeDtypeStruct((total, width), bf16),
+            jax.ShapeDtypeStruct((total, width), bf16),
+            jax.ShapeDtypeStruct((total, w_gu.shape[1]), bf16),
+            jax.ShapeDtypeStruct((total, w_down.shape[0]), bf16),
+        ),
+        in_specs=[vmem] * 5,
+        out_specs=(vmem,) * 4,
+        scratch_shapes=[
+            pltpu.VMEM((total, 128), jnp.float32),
+            pltpu.SemaphoreType.DMA((2, n - 1, 3)),
+            pltpu.SemaphoreType.DMA((2, n - 1, 3)),
+        ],
+        compiler_params=pltpu.CompilerParams(
+            collective_id=1, has_side_effects=True, vmem_limit_bytes=48 * 1024 * 1024
+        ),
+    )(tokens, out_grad, weight, w_gu, w_down)
+
+
 def per_device(tokens, out_grad, expert_ids, route_probs, gate_weight, up_weight, down_weight):
     width = tokens.shape[1]
     exp_dev, _, hid = gate_weight.shape
@@ -225,14 +341,18 @@
     columns = jnp.arange(experts, dtype=jnp.int32)
     hit = expert_ids[:, :, None] == columns[None, None, :]
     weight = jnp.sum(jnp.where(hit, route_probs[:, :, None], 0.0), axis=1)
+    w_gate = jnp.concatenate([gate_weight[e] for e in range(exp_dev)], axis=1)
+    w_up = jnp.concatenate([up_weight[e] for e in range(exp_dev)], axis=1)
+    w_down = down_weight.reshape(exp_dev * hid, width)
+    if exp_dev == 2 and lax.axis_size("dp") == 4 and n_owner == 8:
+        w_gu = jnp.concatenate([w_gate, w_up], axis=1)
+        x, dy, dgu, act = gather_call(tokens, out_grad, weight, w_gu, w_down, n_owner)
+        return reduce_call(x.T, dy, dgu, act.T, w_gu, n_owner, tokens.shape[0])
     first = lax.axis_index("expert") * exp_dev
     all_weight = lax.all_gather(weight, "expert", axis=0, tiled=True)
     mine = lax.dynamic_slice_in_dim(all_weight, first, exp_dev, axis=1)
     x = lax.all_gather(tokens, "expert", axis=0, tiled=True)
     dy = lax.all_gather(out_grad, "expert", axis=0, tiled=True)
-    w_gate = jnp.concatenate([gate_weight[e] for e in range(exp_dev)], axis=1)
-    w_up = jnp.concatenate([up_weight[e] for e in range(exp_dev)], axis=1)
-    w_down = down_weight.reshape(exp_dev * hid, width)
     prob = jnp.repeat(mine, hid, axis=1)
     gate = contract(x, w_gate, 1, 0)
     up = contract(x, w_up, 1, 0)
@@ -243,14 +363,6 @@
     act = (silu * up * prob).astype(bf16)
     dgate = (dh * slope).astype(bf16)
     dup = (dh * silu).astype(bf16)
-    if exp_dev == 2 and lax.axis_size("dp") == 4 and n_owner == 8:
-        in_grad, gu, down = reduce_call(
-            x.T, dy, jnp.concatenate([dgate, dup], axis=1), act.T,
-            jnp.concatenate([w_gate, w_up], axis=1), n_owner, tokens.shape[0],
-        )
-        gu = gu.reshape(width // 4, 2, exp_dev, hid)
-        grad_g, grad_u = (gu[:, k].transpose(1, 0, 2) for k in range(2))
-        return (in_grad, grad_g, grad_u, down)
     grad_d = contract(act, dy, 0, 0).astype(bf16).reshape(exp_dev, hid, width)
     grad_g = contract(x, dgate, 0, 0).astype(bf16)
     grad_u = contract(x, dup, 0, 0).astype(bf16)

time: 236 us -> 217 us (0.919)
  Pallas kernels: 92.6 us -> 193 us
  waiting for transfers between devices: 64.9 us -> 0 us
  matrix products: 20 us -> 0 us
  blocking collectives: 15.7 us -> 0 us
  between operations: 14.1 us -> 0.7 us
  local copies, waits for them, and re-layouts: 22.6 us -> 19.1 us
    pallas_call x0 -> x1, Pallas kernels: none -> 101 us  [gather_call(): pl.pallas_call(functools.partial(gather_kernel, n), out_shape=(jax.ShapeD...]
    all_gather x2 -> x0, waiting for transfers between devices: 64.2 us -> none  [the longest x1 38.8 us: per_device(): dy = lax.all_gather(out_grad, 'expert', axis=0, tiled=True)]
    dot_general x3 -> x0, matrix products: 20 us -> none  [contract(): lax.dot_general(left, right, (((left_dim,), (right_dim,)), ((), ())), pre...]
    all_gather x1 -> x0, blocking collectives: 15.7 us -> none  [per_device(): all_weight = lax.all_gather(weight, 'expert', axis=0, tiled=True)]
    pallas_call x0 -> x2, local copies, waits for them, and re-layouts: none -> 8.01 us  [gather_call(): pl.pallas_call(functools.partial(gather_kernel, n), out_shape=(jax.ShapeD...]
    concatenate x1 -> x0, local copies, waits for them, and re-layouts: 4.67 us -> none  [per_device(): jnp.concatenate([dgate, dup], axis=1)]
    reshape x1 -> x0, local copies, waits for them, and re-layouts: 4.57 us -> none  [per_device(): gu = gu.reshape(width // 4, 2, exp_dev, hid)]
    squeeze x1, local copies, waits for them, and re-layouts: 0.32 us -> 3.47 us  [per_device(): w_up = jnp.concatenate([up_weight[e] for e in range(exp_dev)], axis=1)]
  transfers between devices with their start and end apart: 2 -> 0, of which waited for: 2 -> 0; matrix products, arithmetic and copies ran while one was open for 6% -> 0% of each run, Pallas kernels for 0% -> 0%
where the time goes in v3:
time: 217 us
  Pallas kernels  193 us (89%)
  local copies, waits for them, and re-layouts  19.1 us (9%)
  other arithmetic  3.85 us (2%)
    pallas_call x1, Pallas kernels, gather_call(): pl.pallas_call(functools.partial(gather_kernel, n), out_shape=(jax.ShapeD...  101 us
    pallas_call x1, Pallas kernels, reduce_call(): pl.pallas_call(functools.partial(reduce_kernel, n), out_shape=(jax.ShapeD...  91.8 us
    pallas_call x2, local copies, waits for them, and re-layouts, gather_call(): pl.pallas_call(functools.partial(gather_kernel, n), out_shape=(jax.ShapeD...  8.01 us
    unnamed x14, local copies, waits for them, and re-layouts  7.5 us

profile of v3, /device:TPU:0, one launch (start us, length us, event | category | flops | bytes accessed | tf_op | source)
XLA Modules:
  0.0 216.8 jit_solution(10947506723552585526)
XLA Ops:
  0.6 0.7 select_reduce_fusion
  1.4 0.1 copy.15
  1.5 3.5 %slice_bitcast_fusion.1 = (bf16[2048,384]{1,0:T(8,128)(2,1)S(1)}, bf16[2048,384]{1,0:T(8,128)(2,1)S(1)}, bf16[2048,384]{1,0:T(8,128)(2,1)S(1)}, bf16[2048,384]{1,0:T(8,128)(2,1)S(1)}) fusion(bf16[2,2048,384]{2,1,0:T(8,128)(2,1)} %param.12, bf16[2,2048,384]{2,1,0:T(8,128)(2,1)} %param.11), kind=kLoop, calls=%fused_computation.2 | loop fusion | bytes 12582912 | tf_op jit(solution)/shard_map/squeeze | solution.py:345
  4.9 0.0 copy-start.1
  4.9 0.0 copy-start.2
  5.0 3.1 %pad_maximum_fusion.w_ref = bf16[2048,1536]{1,0:T(8,128)(2,1)} fusion(bf16[2048,384]{1,0:T(8,128)(2,1)S(1)} %get-tuple-element.15, bf16[2048,384]{1,0:T(8,128)(2,1)S(1)} %get-tuple-element.14, bf16[2048,384]{1,0:T(8,128)(2,1)S(1)} %get-tuple-element.16, bf16[2048,384]{1,0:T(8,128)(2,1)S(1)} %get-tuple-element.17), kind=kLoop, calls=%fused_computation | loop fusion | flops 25165824 | bytes 12582912 | tf_op jit(solution)/shard_map/concatenate | solution.py:348
  8.1 0.0 copy-done.1
  8.1 0.0 copy-done.2
  8.1 101.4 %shard_map.102 = (bf16[1024,2048]{1,0:T(8,128)(2,1)}, bf16[1024,2048]{1,0:T(8,128)(2,1)}, bf16[1024,1536]{1,0:T(8,128)(2,1)S(1)}, bf16[1024,768]{1,0:T(8,128)(2,1)S(1)}) custom-call(bf16[128,2048]{1,0:T(8,128)(2,1)S(1)} %copy-done.1, bf16[128,2048]{1,0:T(8,128)(2,1)S(1)} %copy-done.2, f32[128,128]{1,0:T(8,128)S(1)} %pad.4.own_wt_ref, ...), custom_call_target="tpu_custom_call" | custom-call | tf_op jit(solution)/shard_map/pallas_call | solution.py:314
  109.5 0.0 copy-start
  109.5 1.6 copy-done
  111.1 6.4 %copy.16 = bf16[1024,2048]{0,1:T(8,128)(2,1)} copy(bf16[1024,2048]{1,0:T(8,128)(2,1)} %get-tuple-element.8) | data formatting | bytes 8388608 | tf_op jit(solution)/shard_map/pallas_call | solution.py:314
  117.5 1.6 copy.17
  119.2 91.8 %shard_map.103 = (bf16[128,2048]{1,0:T(8,128)(2,1)}, bf16[2,512,384]{2,1,0:T(8,128)(2,1)}, bf16[2,512,384]{2,1,0:T(8,128)(2,1)}, bf16[2,384,512]{2,1,0:T(8,128)(2,1)}) custom-call(bf16[2048,1024]{1,0:T(8,128)(2,1)} %bitcast.11, bf16[1024,2048]{1,0:T(8,128)(2,1)} %get-tuple-element.9.dy_ref, bf16[1024,1536]{1,0:T(8,128)(2,1)} %copy-done, ...), custom_call_target="tpu_custom_call" | custom-call | tf_op jit(solution)/shard_map/pallas_call | solution.py:193
  211.0 0.0 copy-start.4
  211.0 0.0 copy-start.3
  211.0 2.0 copy.22
  213.0 2.1 copy.23
  215.1 0.0 copy-done.4
  215.1 0.9 copy.24
  215.9 0.0 copy-done.3
  216.0 0.9 copy.25
  (1 shorter events, 0.0 us)
Async XLA Ops:
  4.9 3.2 %copy-start.1 = (bf16[128,2048]{1,0:T(8,128)(2,1)S(1)}, bf16[128,2048]{1,0:T(8,128)(2,1)}, u32[]{:S(2)}) copy-start(bf16[128,2048]{1,0:T(8,128)(2,1)} %tok_ref.1) | copy-start | bytes 1572868
  4.9 3.2 %copy-start.2 = (bf16[128,2048]{1,0:T(8,128)(2,1)S(1)}, bf16[128,2048]{1,0:T(8,128)(2,1)}, u32[]{:S(2)}) copy-start(bf16[128,2048]{1,0:T(8,128)(2,1)} %own_dy_ref.1) | copy-start | bytes 1572868
  109.5 1.6 copy-start
  211.0 4.1 %copy-start.4 = (bf16[2,512,384]{2,1,0:T(8,128)(2,1)S(1)}, bf16[2,512,384]{2,1,0:T(8,128)(2,1)}, u32[]{:S(2)}) copy-start(bf16[2,512,384]{2,1,0:T(8,128)(2,1)} %get-tuple-element.24) | copy-start | bytes 2359300
  211.0 5.0 %copy-start.3 = (bf16[2,384,512]{2,1,0:T(8,128)(2,1)S(1)}, bf16[2,384,512]{2,1,0:T(8,128)(2,1)}, u32[]{:S(2)}) copy-start(bf16[2,384,512]{2,1,0:T(8,128)(2,1)} %get-tuple-element.25) | copy-start | bytes 2359300
